TPU v7x, 512 devices: a whole 4x8x8 slice. The times are simulated.
512 devices in a mesh: dp: 8 (over y), seq: 64 (over z, x, core).
Axes of the slice: x: 4, y: 8, z: 8, core: 2. Of those that a mesh axis runs over, the one named last changes fastest.
Arguments:
- tokens: bfloat16 [8, 32768, 1024], P('dp', 'seq'), may hold values from -50 to 50
- w_query: bfloat16 [1024, 1024], P(None, 'dp'), may hold values from -0.1875 to 0.1875
- w_key: bfloat16 [1024, 1024], P(None, 'dp'), may hold values from -0.1875 to 0.1875
- w_value: bfloat16 [1024, 1024], P(None, 'dp'), may hold values from -0.1875 to 0.1875
- w_out: bfloat16 [1024, 1024], P('dp'), may hold values from -0.1875 to 0.1875
- norm_gain: float32 [1024], replicated, may hold values from 0.1 to 1.9
Outputs:
- layer_out: bfloat16 [8, 32768, 1024], P('dp', 'seq')
All inputs are finite; a program needn't handle non-finite values.
Results may differ from a plain program's by a relative error of at most 0.017.
Values may be sent and summed in bfloat16 or wider, within the bound.
No kernel may reach another device: no remote copies, remote signals or barrier semaphores. Data moves between devices by JAX's collectives and lax.ppermute only.
A program may use at most 128 MiB of HBM per device.

v0:
```python
import jax
import jax.numpy as jnp
from jax import lax
from jax.sharding import PartitionSpec as P

H = 8
DH = 128


def entering(value, axis, join, neutral):
    place = lax.axis_index(axis)
    gathered = lax.all_gather(value.astype(jnp.bfloat16), axis)
    state = jnp.zeros_like(value) + jnp.asarray(neutral, value.dtype)

    def one(lap, state):
        return join(state, lax.dynamic_index_in_dim(gathered, lap, 0, False).astype(value.dtype))

    return lax.fori_loop(0, place, one, state)


def inner_block(query_heads, key_heads, value_heads):
    length = query_heads.shape[1]
    block = min(length, 512)
    scores = jnp.einsum("hid,hjd->hij", query_heads, key_heads, preferred_element_type=jnp.float32)
    row_ids = jnp.arange(0, block)[:, None]
    col_ids = jnp.arange(block)[None, :]
    scores = jnp.where(col_ids <= row_ids, scores, 0.0).astype(jnp.bfloat16)
    pieces = jnp.einsum("hij,hje->hie", scores, value_heads, preferred_element_type=jnp.float32)
    return pieces


def add_states(earlier, later):
    return earlier + later


def key_value_state(key_heads, value_heads):
    return jnp.einsum("htd,hte->hde", key_heads, value_heads, preferred_element_type=jnp.float32)


def attend(query_heads, key_heads, value_heads, prior):
    within = inner_block(query_heads, key_heads, value_heads)
    carried = jnp.einsum(
        "htd,hde->hte", query_heads, prior.astype(jnp.bfloat16), preferred_element_type=jnp.float32
    )
    return within + carried


def body(tokens, w_query, w_key, w_value, w_out, norm_gain):
    rows = tokens[0]
    length = rows.shape[0]
    full_query, full_key, full_value = (
        lax.all_gather(w_query, "dp", axis=1, tiled=True),
        lax.all_gather(w_key, "dp", axis=1, tiled=True),
        lax.all_gather(w_value, "dp", axis=1, tiled=True),
    )
    query = jnp.dot(rows, full_query, preferred_element_type=jnp.float32).astype(jnp.bfloat16)
    key = jnp.dot(rows, full_key, preferred_element_type=jnp.float32).astype(jnp.bfloat16)
    value = jnp.dot(rows, full_value, preferred_element_type=jnp.float32).astype(jnp.bfloat16)
    query_heads = query.reshape(length, H, DH).transpose(1, 0, 2)
    key_heads = key.reshape(length, H, DH).transpose(1, 0, 2)
    value_heads = value.reshape(length, H, DH).transpose(1, 0, 2)
    local_state = key_value_state(key_heads, value_heads)
    empty_state = jnp.zeros((H, DH, DH), jnp.float32)
    prior = entering(local_state, "seq", add_states, empty_state)
    mixed_raw = attend(query_heads, key_heads, value_heads, prior)
    scale = lax.rsqrt(jnp.mean(mixed_raw * mixed_raw, axis=-1, keepdims=True) + 1e-05)
    normed = (mixed_raw * scale * norm_gain.reshape(H, 1, DH)).astype(jnp.bfloat16)
    normed = normed.transpose(1, 0, 2).reshape(length, H * DH)
    result = jnp.dot(
        normed, lax.all_gather(w_out, "dp", axis=0, tiled=True), preferred_element_type=jnp.float32
    )
    return result.astype(jnp.bfloat16)[None]


def solution(mesh):
    in_specs = (
        P("dp", "seq", None),
        P(None, "dp"),
        P(None, "dp"),
        P(None, "dp"),
        P("dp", None),
        P(),
    )
    out_specs = P("dp", "seq", None)
    return jax.shard_map(body, mesh=mesh, in_specs=in_specs, out_specs=out_specs, check_vma=False)
```

profile of v0, /device:TPU:455, one launch (start us, length us, event | category | flops | bytes accessed | tf_op | source)
XLA Modules:
  0.0 347.7 jit_solution(2035250541791715043)
XLA Ops:
  8.8 46.0 %all-gather.9.cloned.1.call-done = bf16[1024,1024]{1,0:T(8,128)(2,1)} async-done(((bf16[1024,128]{1,0:T(8,128)(2,1)}), bf16[1024,1024]{1,0:T(8,128)(2,1)}) %all-gather.9.cloned.1.call-update) | async-done | bytes 2097168 | tf_op jit(solution)/shard_map/all_gather | solution.py:53
  54.8 2.8 convolution_convert_fusion.2
  58.2 47.8 %all-gather.11.cloned.1.call-done = bf16[1024,1024]{1,0:T(8,128)(2,1)} async-done(((bf16[1024,128]{1,0:T(8,128)(2,1)}), bf16[1024,1024]{1,0:T(8,128)(2,1)}) %all-gather.11.cloned.1.call-update) | async-done | bytes 2097168 | tf_op jit(solution)/shard_map/all_gather | solution.py:54
  106.0 2.8 convolution_convert_fusion.1
  108.8 1.2 convolution_convert_fusion.4
  110.8 1.2 copy.24
  112.0 45.2 %all-gather.7.cloned.1.call-done = bf16[1024,1024]{1,0:T(8,128)(2,1)} async-done(((bf16[1024,128]{1,0:T(8,128)(2,1)}), bf16[1024,1024]{1,0:T(8,128)(2,1)}) %all-gather.7.cloned.1.call-update) | async-done | bytes 2097168 | tf_op jit(solution)/shard_map/all_gather | solution.py:52
  157.2 3.8 %fusion.7 = bf16[64,8,8,128]{3,2,1,0:T(8,128)(2,1)} fusion(bf16[1024,1024]{1,0:T(8,128)(2,1)} %all-gather.7.cloned.1.call-done, bf16[1,512,1024]{2,1,0:T(8,128)(2,1)S(1)} %copy-done), kind=kOutput, calls=%fused_computation.15 | convolution fusion | flops 1074266112 | bytes 4194304 | tf_op jit(solution)/shard_map/dot_general | solution.py:56
  161.0 5.1 %fusion = f32[8,512,128]{1,2,0:T(8,128)} fusion(pred[512,512]{1,0:T(8,128)(4,1)S(1)} %iota_compare_fusion, bf16[8,512,128]{1,2,0:T(8,128)(2,1)S(1)} %bitcast.67, bf16[8,512,128]{2,0,1:T(8,128)(2,1)S(1)} %bitcast.69, bf16[64,8,8,128]{3,2,1,0:T(8,128)(2,1)} %fusion.7), kind=kOutput, calls=%fused_computation.2 | convolution fusion | flops 1077936128 | bytes 5505024 | tf_op jit(solution)/shard_map/hij,hje->hie/dot_general | solution.py:28
  166.1 99.4 %all-gather.15.cloned.1.call-done = bf16[512,128,128]{2,1,0:T(8,128)(2,1)} async-done(((bf16[8,128,128]{2,1,0:T(8,128)(2,1)}), bf16[512,128,128]{2,1,0:T(8,128)(2,1)}) %all-gather.15.cloned.1.call-update) | async-done | bytes 16777232 | tf_op jit(solution)/shard_map/all_gather | solution.py:12
  265.6 69.2 %while.10 = (s32[]{:T(128)}, f32[8,128,128]{2,1,0:T(8,128)S(1)}, s32[]{:T(128)}, bf16[64,8,128,128]{3,2,1,0:T(8,128)(2,1)}, s32[]{:T(128)}, /*index=5*/s32[]{:T(128)}, s32[]{:T(128)}) while((s32[]{:T(128)}, f32[8,128,128]{2,1,0:T(8,128)S(1)}, s32[]{:T(128)}, bf16[64,8,128,128]{3,2,1,0:T(8,128)(2,1)}, s32[]{:T(128)}, /*index=5*/s32[]{:T(128)}, ...), condition=%wide.region_1.2_spmd, body=%wide.region_0.1_spmd.sunk | while | flops 262149 | bytes 1310835 | solution.py:18
  265.6 1.2 convert_add_fusion.2
  266.8 1.1 convert_add_fusion.2
  267.9 1.1 convert_add_fusion.2
  269.0 1.1 convert_add_fusion.2
  270.1 1.1 convert_add_fusion.2
  271.2 1.1 convert_add_fusion.2
  272.3 1.1 convert_add_fusion.2
  273.4 1.1 convert_add_fusion.2
  274.5 1.1 convert_add_fusion.2
  275.6 1.1 convert_add_fusion.2
  276.7 1.1 convert_add_fusion.2
  277.8 1.1 convert_add_fusion.2
  278.9 1.1 convert_add_fusion.2
  280.0 1.1 convert_add_fusion.2
  281.1 1.1 convert_add_fusion.2
  282.2 1.1 convert_add_fusion.2
  285.4 1.1 convert_add_fusion.2
  286.5 1.1 convert_add_fusion.2
  287.6 1.1 convert_add_fusion.2
  288.7 1.1 convert_add_fusion.2
  290.9 1.1 convert_add_fusion.2
  292.0 1.1 convert_add_fusion.2
  293.1 1.1 convert_add_fusion.2
  294.2 1.1 convert_add_fusion.2
  295.3 1.1 convert_add_fusion.2
  296.4 1.1 convert_add_fusion.2
  297.5 1.1 convert_add_fusion.2
  298.6 1.1 convert_add_fusion.2
  299.7 1.1 convert_add_fusion.2
  300.8 1.1 convert_add_fusion.2
  301.9 1.1 convert_add_fusion.2
  303.0 1.1 convert_add_fusion.2
  305.2 1.1 convert_add_fusion.2
  306.3 1.1 convert_add_fusion.2
  307.4 1.1 convert_add_fusion.2
  310.7 1.1 convert_add_fusion.2
  311.8 1.1 convert_add_fusion.2
  312.9 1.1 convert_add_fusion.2
  315.1 1.1 convert_add_fusion.2
  316.2 1.1 convert_add_fusion.2
  317.3 1.1 convert_add_fusion.2
  318.4 1.1 convert_add_fusion.2
  320.6 1.1 convert_add_fusion.2
  321.7 1.1 convert_add_fusion.2
  322.8 1.1 convert_add_fusion.2
  326.0 1.1 convert_add_fusion.2
  327.1 1.1 convert_add_fusion.2
  328.2 1.1 convert_add_fusion.2
  331.5 1.1 convert_add_fusion.2
  332.6 1.1 convert_add_fusion.2
  333.7 1.1 convert_add_fusion.2
  334.8 2.1 multiply_reduce_fusion
  337.4 3.8 %fusion.8 = bf16[1,512,1024]{2,1,0:T(8,128)(2,1)} fusion(bf16[512,1024]{0,1:T(8,128)(2,1)S(1)} %bitcast.65, bf16[1024,1024]{1,0:T(8,128)(2,1)} %all-gather.13.cloned.1.call-done), kind=kOutput, calls=%fused_computation.16 | convolution fusion | flops 1074266112 | bytes 4194304 | tf_op jit(solution)/shard_map/dot_general | solution.py:69
  (36 shorter events, 16.7 us)
Async XLA Ops:
  6.5 48.3 %copy-start = (bf16[1,512,1024]{2,1,0:T(8,128)(2,1)S(1)}, bf16[1,512,1024]{2,1,0:T(8,128)(2,1)}, u32[]{:S(2)}) copy-start(bf16[1,512,1024]{2,1,0:T(8,128)(2,1)} %param.8) | copy-start | bytes 3145732
  6.5 48.3 %all-gather.9.cloned.1.call-start = ((), (), s32[]{:S(2)}) async-start(), calls=%async_computation.1 | async-start | bytes 2359296 | tf_op jit(solution)/shard_map/all_gather | solution.py:53
  7.3 98.7 %all-gather.11.cloned.1.call-start = ((), (), s32[]{:S(2)}) async-start(), calls=%async_computation.2 | async-start | bytes 2359296 | tf_op jit(solution)/shard_map/all_gather | solution.py:54
  8.0 149.2 %all-gather.7.cloned.1.call-start = ((), (), s32[]{:S(2)}) async-start(), calls=%async_computation | async-start | bytes 2359296 | tf_op jit(solution)/shard_map/all_gather | solution.py:52
  8.7 256.8 %all-gather.15.cloned.1.call-start = ((), (), s32[]{:S(2)}) async-start(), calls=%async_computation.4 | async-start | bytes 17039360 | tf_op jit(solution)/shard_map/all_gather | solution.py:12
  110.1 227.3 %all-gather.13.cloned.1.call-start = ((), (), s32[]{:S(2)}) async-start(), calls=%async_computation.3 | async-start | bytes 2359296 | tf_op jit(solution)/shard_map/all_gather | solution.py:70
  112.0 49.0 %copy-start.1 = (bf16[64,8,8,128]{3,2,1,0:T(8,128)(2,1)S(1)}, bf16[64,8,8,128]{3,2,1,0:T(8,128)(2,1)}, u32[]{:S(2)}) copy-start(bf16[64,8,8,128]{3,2,1,0:T(8,128)(2,1)} %copy.24) | copy-start | bytes 3145732
  265.6 69.2 %copy-start.2 = (bf16[64,8,8,128]{3,2,1,0:T(8,128)(2,1)S(1)}, bf16[64,8,8,128]{3,2,1,0:T(8,128)(2,1)}, u32[]{:S(2)}) copy-start(bf16[64,8,8,128]{3,2,1,0:T(8,128)(2,1)} %fusion.7) | copy-start | bytes 3145732
  334.8 2.2 copy-start.3
Sparse Core Ops, SparseCore 0:
  9.4 45.3 all-gather.8
  56.8 49.1 all-gather.10
  108.0 49.1 all-gather.6
  160.4 105.0 all-gather.14
  267.5 40.4 all-gather.12
where the time goes:
time: 350 us; the launch traced here: 348 us
  waiting for transfers between devices  241 us (69%)
  other arithmetic  67.9 us (19%)
  matrix products  21.8 us (6%)
  between operations  13.2 us (4%)
    all_gather x1, waiting for transfers between devices, entering(): gathered = lax.all_gather(value.astype(jnp.bfloat16), axis)  99.4 us
    add x63, other arithmetic, add_states(): return earlier + later  67.5 us
    all_gather x1, waiting for transfers between devices, body(): lax.all_gather(w_value, 'dp', axis=1, tiled=True)  47.8 us
    all_gather x1, waiting for transfers between devices, body(): lax.all_gather(w_key, 'dp', axis=1, tiled=True)  46 us
    all_gather x1, waiting for transfers between devices, body(): lax.all_gather(w_query, 'dp', axis=1, tiled=True)  45.2 us
  transfers between devices with their start and end apart: 5, of which 4 were waited for; matrix products, arithmetic and copies ran while one was open for 25% of the time, Pallas kernels for 0%

commit v1 on v0

--- a/solution.py
+++ b/solution.py
@@ -48,9 +48,17 @@
 def body(tokens, w_query, w_key, w_value, w_out, norm_gain):
     rows = tokens[0]
     length = rows.shape[0]
+
+    def samples_all_supply_all(arr_in, ax_name, on_dim):
+        pile = []
+        for _ in range(jax.lax.axis_size(ax_name)):
+            pile.append(arr_in)
+        all_values = jnp.concatenate(pile, axis=on_dim)
+        return jax.lax.all_to_all(all_values, ax_name, on_dim, on_dim, tiled=True)
+
     full_query, full_key, full_value = (
         lax.all_gather(w_query, "dp", axis=1, tiled=True),
-        lax.all_gather(w_key, "dp", axis=1, tiled=True),
+        samples_all_supply_all(w_key, "dp", on_dim=1),
         lax.all_gather(w_value, "dp", axis=1, tiled=True),
     )
     query = jnp.dot(rows, full_query, preferred_element_type=jnp.float32).astype(jnp.bfloat16)

time: 350 us -> 331 us (0.946)
  waiting for transfers between devices: 241 us -> 211 us
  starting transfers between devices: 0.16 us -> 6.94 us
  local copies, waits for them, and re-layouts: 1.84 us -> 6.57 us
    all_to_all x0 -> x1, waiting for transfers between devices: none -> 63.6 us  [samples_all_supply_all(): return jax.lax.all_to_all(all_values, ax_name, on_dim, on_dim, tiled=True)]
    all_gather x1 -> x0, waiting for transfers between devices: 46 us -> none  [body(): lax.all_gather(w_key, 'dp', axis=1, tiled=True)]
    all_gather x1, waiting for transfers between devices: 47.8 us -> 4.98 us  [body(): lax.all_gather(w_value, 'dp', axis=1, tiled=True)]
    all_to_all x0 -> x1, starting transfers between devices: none -> 6.82 us  [samples_all_supply_all(): return jax.lax.all_to_all(all_values, ax_name, on_dim, on_dim, tiled=True)]
    all_gather x1, waiting for transfers between devices: 45.2 us -> 39.9 us  [body(): lax.all_gather(w_query, 'dp', axis=1, tiled=True)]
    all_to_all x0 -> x2, local copies, waits for them, and re-layouts: none -> 5 us  [samples_all_supply_all(): return jax.lax.all_to_all(all_values, ax_name, on_dim, on_dim, tiled=True)]
  transfers between devices with their start and end apart: 5 -> 5, of which waited for: 4 -> 4; matrix products, arithmetic and copies ran while one was open for 25% -> 28% of each run, Pallas kernels for 0% -> 0%
where the time goes in v1:
time: 331 us; the launch traced here: 328 us
  waiting for transfers between devices  211 us (64%)
  other arithmetic  67.9 us (21%)
  matrix products  21.2 us (6%)
  between operations  13.3 us (4%)
  starting transfers between devices  6.94 us (2%)
  local copies, waits for them, and re-layouts  6.57 us (2%)
    all_gather x1, waiting for transfers between devices, entering(): gathered = lax.all_gather(value.astype(jnp.bfloat16), axis)  100 us
    add x63, other arithmetic, add_states(): return earlier + later  67.5 us
    all_to_all x1, waiting for transfers between devices, samples_all_supply_all(): return jax.lax.all_to_all(all_values, ax_name, on_dim, on_dim, tiled=True)  63.6 us
    all_gather x1, waiting for transfers between devices, body(): lax.all_gather(w_query, 'dp', axis=1, tiled=True)  39.9 us
    all_to_all x1, starting transfers between devices, samples_all_supply_all(): return jax.lax.all_to_all(all_values, ax_name, on_dim, on_dim, tiled=True)  6.82 us
  transfers between devices with their start and end apart: 5, of which 4 were waited for; matrix products, arithmetic and copies ran while one was open for 28% of the time, Pallas kernels for 0%

profile of v1, /device:TPU:455, one launch (start us, length us, event | category | flops | bytes accessed | tf_op | source)
XLA Modules:
  0.0 328.2 jit_solution(16063447791426921677)
XLA Ops:
  7.3 1.1 copy.16
  8.6 2.4 copy.24
  11.0 6.8 %all-to-all-start = ((bf16[1024,8,128]{2,0,1:T(8,128)(2,1)}), bf16[1024,8,128]{2,0,1:T(8,128)(2,1)S(1)}, u32[]{:S(2)}, u32[]{:S(2)}) async-start(bf16[1024,8,128]{2,0,1:T(8,128)(2,1)} %copy.24), calls=%async_computation | async-start | bytes 4194304 | tf_op jit(solution)/shard_map/all_to_all | solution.py:57
  18.6 63.6 %all-to-all-done = bf16[1024,8,128]{2,0,1:T(8,128)(2,1)S(1)} async-done(((bf16[1024,8,128]{2,0,1:T(8,128)(2,1)}), bf16[1024,8,128]{2,0,1:T(8,128)(2,1)S(1)}, u32[]{:S(2)}, u32[]{:S(2)}) %all-to-all-start) | async-done | bytes 2097184 | tf_op jit(solution)/shard_map/all_to_all | solution.py:57
  82.1 2.6 copy.25
  84.7 2.9 convolution_convert_fusion.2
  87.6 5.0 %all-gather.8.cloned.1.call-done = bf16[1024,1024]{1,0:T(8,128)(2,1)} async-done(((bf16[1024,128]{1,0:T(8,128)(2,1)}), bf16[1024,1024]{1,0:T(8,128)(2,1)}) %all-gather.8.cloned.1.call-update) | async-done | bytes 2097168 | tf_op jit(solution)/shard_map/all_gather | solution.py:62
  92.6 2.8 convolution_convert_fusion.1
  95.5 1.2 convolution_convert_fusion.4
  97.6 39.9 %all-gather.6.cloned.1.call-done = bf16[1024,1024]{1,0:T(8,128)(2,1)} async-done(((bf16[1024,128]{1,0:T(8,128)(2,1)}), bf16[1024,1024]{1,0:T(8,128)(2,1)}) %all-gather.6.cloned.1.call-update) | async-done | bytes 2097168 | tf_op jit(solution)/shard_map/all_gather | solution.py:60
  137.6 2.8 fusion.7
  140.4 5.5 %fusion = f32[8,512,128]{1,2,0:T(8,128)} fusion(pred[512,512]{1,0:T(8,128)(4,1)S(1)} %iota_compare_fusion, bf16[8,512,128]{1,2,0:T(8,128)(2,1)} %bitcast.77, bf16[8,512,128]{2,0,1:T(8,128)(2,1)S(1)} %bitcast.73, bf16[64,8,8,128]{3,2,1,0:T(8,128)(2,1)S(1)} %fusion.7), kind=kOutput, calls=%fused_computation.2 | convolution fusion | flops 1077936128 | bytes 5505024 | tf_op jit(solution)/shard_map/hij,hje->hie/dot_general | solution.py:28
  146.0 100.1 %all-gather.12.cloned.1.call-done = bf16[512,128,128]{2,1,0:T(8,128)(2,1)} async-done(((bf16[8,128,128]{2,1,0:T(8,128)(2,1)}), bf16[512,128,128]{2,1,0:T(8,128)(2,1)}) %all-gather.12.cloned.1.call-update) | async-done | bytes 16777232 | tf_op jit(solution)/shard_map/all_gather | solution.py:12
  246.1 69.2 %while.10 = (s32[]{:T(128)}, f32[8,128,128]{2,1,0:T(8,128)S(1)}, s32[]{:T(128)}, bf16[64,8,128,128]{3,2,1,0:T(8,128)(2,1)}, s32[]{:T(128)}, /*index=5*/s32[]{:T(128)}, s32[]{:T(128)}) while((s32[]{:T(128)}, f32[8,128,128]{2,1,0:T(8,128)S(1)}, s32[]{:T(128)}, bf16[64,8,128,128]{3,2,1,0:T(8,128)(2,1)}, s32[]{:T(128)}, /*index=5*/s32[]{:T(128)}, ...), condition=%wide.region_1.2_spmd, body=%wide.region_0.1_spmd.sunk | while | flops 262149 | bytes 1310835 | solution.py:18
  246.2 1.2 convert_add_fusion.2
  247.3 1.1 convert_add_fusion.2
  249.5 1.1 convert_add_fusion.2
  250.6 1.1 convert_add_fusion.2
  251.7 1.1 convert_add_fusion.2
  252.8 1.1 convert_add_fusion.2
  255.0 1.1 convert_add_fusion.2
  256.1 1.1 convert_add_fusion.2
  257.2 1.1 convert_add_fusion.2
  260.5 1.1 convert_add_fusion.2
  261.6 1.1 convert_add_fusion.2
  262.7 1.1 convert_add_fusion.2
  263.8 1.1 convert_add_fusion.2
  264.9 1.1 convert_add_fusion.2
  266.0 1.1 convert_add_fusion.2
  268.2 1.1 convert_add_fusion.2
  269.3 1.1 convert_add_fusion.2
  270.4 1.1 convert_add_fusion.2
  271.5 1.1 convert_add_fusion.2
  272.6 1.1 convert_add_fusion.2
  274.8 1.1 convert_add_fusion.2
  275.9 1.1 convert_add_fusion.2
  277.0 1.1 convert_add_fusion.2
  278.1 1.1 convert_add_fusion.2
  279.2 1.1 convert_add_fusion.2
  280.3 1.1 convert_add_fusion.2
  281.4 1.1 convert_add_fusion.2
  282.5 1.1 convert_add_fusion.2
  283.6 1.1 convert_add_fusion.2
  286.8 1.1 convert_add_fusion.2
  287.9 1.1 convert_add_fusion.2
  289.0 1.1 convert_add_fusion.2
  291.2 1.1 convert_add_fusion.2
  292.3 1.1 convert_add_fusion.2
  293.4 1.1 convert_add_fusion.2
  294.5 1.1 convert_add_fusion.2
  296.7 1.1 convert_add_fusion.2
  297.8 1.1 convert_add_fusion.2
  298.9 1.1 convert_add_fusion.2
  302.2 1.1 convert_add_fusion.2
  303.3 1.1 convert_add_fusion.2
  304.4 1.1 convert_add_fusion.2
  307.7 1.1 convert_add_fusion.2
  308.8 1.1 convert_add_fusion.2
  309.9 1.1 convert_add_fusion.2
  312.1 1.1 convert_add_fusion.2
  313.2 1.1 convert_add_fusion.2
  314.3 1.1 convert_add_fusion.2
  315.4 2.1 multiply_reduce_fusion
  317.9 3.8 %fusion.8 = bf16[1,512,1024]{2,1,0:T(8,128)(2,1)} fusion(bf16[512,1024]{0,1:T(8,128)(2,1)S(1)} %bitcast.69, bf16[1024,1024]{1,0:T(8,128)(2,1)} %all-gather.10.cloned.1.call-done), kind=kOutput, calls=%fused_computation.16 | convolution fusion | flops 1074266112 | bytes 4194304 | tf_op jit(solution)/shard_map/dot_general | solution.py:77
  (47 shorter events, 19.0 us)
Async XLA Ops:
  6.5 78.2 %copy-start = (bf16[1,512,1024]{2,1,0:T(8,128)(2,1)S(1)}, bf16[1,512,1024]{2,1,0:T(8,128)(2,1)}, u32[]{:S(2)}) copy-start(bf16[1,512,1024]{2,1,0:T(8,128)(2,1)} %param.8) | copy-start | bytes 3145732
  6.5 86.1 %all-gather.8.cloned.1.call-start = ((), (), s32[]{:S(2)}) async-start(), calls=%async_computation.2 | async-start | bytes 2359296 | tf_op jit(solution)/shard_map/all_gather | solution.py:62
  11.0 71.2 %all-to-all-start = ((bf16[1024,8,128]{2,0,1:T(8,128)(2,1)}), bf16[1024,8,128]{2,0,1:T(8,128)(2,1)S(1)}, u32[]{:S(2)}, u32[]{:S(2)}) async-start(bf16[1024,8,128]{2,0,1:T(8,128)(2,1)} %copy.24), calls=%async_computation | async-start | bytes 4194304 | tf_op jit(solution)/shard_map/all_to_all | solution.py:57
  17.8 119.8 %all-gather.6.cloned.1.call-start = ((), (), s32[]{:S(2)}) async-start(), calls=%async_computation.1 | async-start | bytes 2359296 | tf_op jit(solution)/shard_map/all_gather | solution.py:60
  18.5 227.5 %all-gather.12.cloned.1.call-start = ((), (), s32[]{:S(2)}) async-start(), calls=%async_computation.4 | async-start | bytes 17039360 | tf_op jit(solution)/shard_map/all_gather | solution.py:12
  87.6 7.8 %copy-start.4 = (bf16[1024,512]{1,0:T(8,128)(2,1)}, bf16[1024,512]{1,0:T(8,128)(2,1)S(1)}, u32[]{:S(2)}) copy-start(bf16[1024,512]{1,0:T(8,128)(2,1)S(1)} %convolution_convert_fusion.2) | copy-start | bytes 3145732
  96.7 221.2 %all-gather.10.cloned.1.call-start = ((), (), s32[]{:S(2)}) async-start(), calls=%async_computation.3 | async-start | bytes 2359296 | tf_op jit(solution)/shard_map/all_gather | solution.py:78
  140.4 5.5 %copy-start.1 = (bf16[64,8,8,128]{3,2,1,0:T(8,128)(2,1)}, bf16[64,8,8,128]{3,2,1,0:T(8,128)(2,1)S(1)}, u32[]{:S(2)}) copy-start(bf16[64,8,8,128]{3,2,1,0:T(8,128)(2,1)S(1)} %fusion.7) | copy-start | bytes 3145732
  246.1 69.2 %copy-start.2 = (bf16[64,8,8,128]{3,2,1,0:T(8,128)(2,1)S(1)}, bf16[64,8,8,128]{3,2,1,0:T(8,128)(2,1)}, u32[]{:S(2)}) copy-start(bf16[64,8,8,128]{3,2,1,0:T(8,128)(2,1)} %copy-done.1) | copy-start | bytes 3145732
  315.3 2.2 copy-start.3
Sparse Core Ops, SparseCore 0:
  9.4 83.2 all-gather.7
  94.6 42.9 all-gather.5
  140.9 105.0 all-gather.11
  248.0 40.4 all-gather.9
